TPU v7x, 32 devices: a whole 2x2x4 slice. The times are simulated.
32 devices in a mesh: patch: 4 (over x, core), proto: 8 (over z, y).
Axes of the slice: x: 2, y: 2, z: 4, core: 2. Of those that a mesh axis runs over, the one named last changes fastest.
Arguments:
- student_feats: bfloat16 [8192, 256], P(('patch', 'proto')), may hold values from -50 to 50
- teacher_feats: bfloat16 [8192, 256], P(('patch', 'proto')), may hold values from -50 to 50
- proto_weight: bfloat16 [256, 131072], P(None, 'proto'), may hold values from -4 to 4
- mask_index: int32 [1024], P(('patch', 'proto')), may hold values from 0 to 255, as said below
- row_weight: bfloat16 [1024], P(('patch', 'proto')), may hold values from 0.5 to 4
Outputs:
- grad_student: float32 [1024, 256], P(('patch', 'proto'))
- grad_proto: float32 [256, 131072], P('patch', 'proto')
- loss: float32 [], replicated
Inputs may be any that keep to these rules, and one draw needn't show every extreme that they name: `mask_index`: entries k * 32 to (k + 1) * 32 - 1 are distinct patch positions of image k, counted from that image's first patch.
All inputs are finite; a program needn't handle non-finite values.
Results may differ from a plain program's by a relative error of at most 0.0057.
Values may be sent and summed in bfloat16 or wider, within the bound.
A program may use at most 128 MiB of HBM per device.

v0:
```python
import jax
import jax.numpy as jnp
from jax import lax
from jax.sharding import PartitionSpec as P

SK_ITERS = 3


eps = 1e-06
teacher_temp = 0.07
student_temp = 0.1


def unit_rows(values):
    values = values.astype(jnp.float32)
    inverse = lax.rsqrt(jnp.sum(values * values, axis=1) + eps)
    return (values * inverse[:, None], inverse)


def finish(teacher_exp, scale_rows, scale_cols, logits, exp_logits, exp_total, weights):
    codes = teacher_exp * scale_rows[:, None] * scale_cols[None, :]
    student_probs = exp_logits / exp_total[:, None]
    grad_logits = (weights[:, None] * (student_probs - codes)).astype(jnp.bfloat16)
    log_total = jnp.log(exp_total)
    loss_partial = jnp.sum(weights[:, None] * codes * (log_total[:, None] - logits))
    return (grad_logits, loss_partial)


def feature_term(grad_logits, proto_cols):
    return (
        lax.dot_general(
            grad_logits, proto_cols, (((1,), (1,)), ((), ())), preferred_element_type=jnp.float32
        )
        / student_temp
    )


def head_term(student_rows, grad_logits):
    return (
        lax.dot_general(
            student_rows, grad_logits, (((0,), (0,)), ((), ())), preferred_element_type=jnp.float32
        )
        / student_temp
    )


def on_device(student_feats, teacher_feats, proto_weight, mask_index, row_weight):
    highest = lax.Precision.HIGHEST
    unit_student, inverse_student = unit_rows(jnp.take(student_feats, mask_index, axis=0))
    unit_teacher, _ = unit_rows(jnp.take(teacher_feats, mask_index, axis=0))
    own_student = unit_student.astype(jnp.bfloat16)
    own_teacher = unit_teacher.astype(jnp.bfloat16)
    w_float = proto_weight.astype(jnp.float32)
    col_inverse = lax.rsqrt(jnp.sum(w_float * w_float, axis=0) + eps)
    unit_proto = w_float * col_inverse[None, :]
    proto_unit = unit_proto.astype(jnp.bfloat16)
    teacher_rows, student_rows, weights = (
        lax.all_gather(own_teacher, "proto", axis=0, tiled=True),
        lax.all_gather(own_student, "proto", axis=0, tiled=True),
        lax.all_gather(row_weight, "proto", axis=0, tiled=True),
    )
    weights = weights.astype(jnp.float32)
    teacher_exp = jnp.exp(
        jnp.dot(teacher_rows, proto_unit, preferred_element_type=jnp.float32) / teacher_temp
    )
    scale_rows = jnp.ones((teacher_rows.shape[0],), jnp.float32)
    for sweep in range(SK_ITERS):
        col_part = jnp.dot(scale_rows, teacher_exp, precision=highest)
        scale_cols = 1.0 / lax.psum(col_part, "patch")
        row_part = jnp.dot(teacher_exp, scale_cols, precision=highest)
        scale_rows = 1.0 / lax.psum(row_part, "proto")
    logits = jnp.dot(student_rows, proto_unit, preferred_element_type=jnp.float32) / student_temp
    exp_logits = jnp.exp(logits)
    exp_total = lax.psum(jnp.sum(exp_logits, axis=1), "proto")
    grad_logits, loss_partial = finish(
        teacher_exp, scale_rows, scale_cols, logits, exp_logits, exp_total, weights
    )
    feature_grad = lax.psum_scatter(
        feature_term(grad_logits, proto_unit), "proto", scatter_dimension=0, tiled=True
    )
    row_share = proto_unit.shape[0] // lax.axis_size("patch")
    row_offset = lax.axis_index("patch") * row_share
    head_part = lax.psum_scatter(
        head_term(student_rows, grad_logits), "patch", scatter_dimension=0, tiled=True
    )
    unit_own = lax.dynamic_slice_in_dim(unit_proto, row_offset, row_share, 0)
    inner = lax.psum(jnp.sum(unit_own * head_part, axis=0), "patch")
    grad_proto = col_inverse[None, :] * (head_part - unit_own * inner[None, :])
    loss_total, weight_total = lax.psum(
        (loss_partial, jnp.sum(row_weight.astype(jnp.float32))), ("patch", "proto")
    )
    grad_student = inverse_student[:, None] * (
        feature_grad - unit_student * jnp.sum(unit_student * feature_grad, axis=1)[:, None]
    )
    return (grad_student, grad_proto, loss_total / weight_total)


def solution(mesh):
    in_specs = (
        P(("patch", "proto"), None),
        P(("patch", "proto"), None),
        P(None, "proto"),
        P(("patch", "proto")),
        P(("patch", "proto")),
    )
    out_specs = (P(("patch", "proto"), None), P("patch", "proto"), P())
    return jax.shard_map(
        on_device, mesh=mesh, in_specs=in_specs, out_specs=out_specs, check_vma=False
    )
```

profile of v0, /device:TPU:0, one launch (start us, length us, event | category | flops | bytes accessed | tf_op | source)
XLA Modules:
  0.0 557.3 jit_solution(14471883861101810782)
XLA Ops:
  11.0 32.3 %all_gather.11 = bf16[256,256]{1,0:T(8,128)(2,1)S(1)} all-gather(bf16[32,256]{1,0:T(8,128)(2,1)S(1)} %get-tuple-element.12), channel_id=1, replica_groups=mesh['patch'=4,'proto'=8] {'proto'}, dimensions={0}, use_global_device_ids=true | all-gather | bytes 147456 | tf_op jit(solution)/shard_map/all_gather | solution.py:58
  48.5 6.7 %fusion = f32[256,16384]{1,0:T(8,128)S(1)} fusion(bf16[256,256]{1,0:T(8,128)(2,1)S(1)} %all_gather.11, f32[16384]{0:T(1024)S(1)} %add_rsqrt_fusion, bf16[256,16384]{1,0:T(8,128)(2,1)} %param.9), kind=kOutput, calls=%fused_computation.4 | convolution fusion | flops 2164260864 | bytes 25362432 | tf_op jit(solution)/shard_map/dot_general | solution.py:64
  55.2 5.7 %copy-done.2 = f32[256,16384]{1,0:T(8,128)} copy-done((f32[256,16384]{1,0:T(8,128)}, f32[256,16384]{1,0:T(8,128)S(1)}, u32[]{:S(2)}) %copy-start.2) | copy-done | bytes 16777240
  60.9 8.6 %fusion.19 = f32[1,16384]{1,0:T(1,128)} fusion(f32[256,16384]{1,0:T(8,128)S(1)} %fusion), kind=kOutput, calls=%fused_computation.40 | convolution fusion | flops 50331648 | bytes 16842752 | tf_op jit(solution)/shard_map/dot_general | solution.py:68
  69.5 32.1 %all-reduce.8.cloned.1.call-done = f32[16384]{0:T(1024)} async-done(((f32[16384]{0:T(1024)}), f32[16384]{0:T(1024)}) %all-reduce.8.cloned.1.call-update) | async-done | bytes 65552 | tf_op jit(solution)/shard_map/psum | solution.py:69
  102.4 16.2 %fusion.22 = f32[1,256]{1,0:T(1,128)S(1)} fusion(f32[256,16384]{1,0:T(8,128)} %copy-done.2, f32[16384,1]{0,1:T(1,128)S(1)} %bitcast.32), kind=kOutput, calls=%fused_computation.49 | convolution fusion | flops 50331648 | bytes 16843776 | tf_op jit(solution)/shard_map/dot_general | solution.py:70
  118.7 21.4 %psum.72 = f32[256]{0:T(256)S(1)} all-reduce(f32[256]{0:T(256)S(1)} %bitcast.35), channel_id=1, replica_groups=mesh['patch'=4,'proto'=8] {'proto'}, use_global_device_ids=true, to_apply=%region_6.8 | all-reduce | flops 256 | bytes 2048 | tf_op jit(solution)/shard_map/psum | solution.py:71
  140.1 12.1 %fusion.23 = f32[1,16384]{1,0:T(1,128)} fusion(f32[256,1]{0,1:T(1,128)S(1)} %bitcast.36, f32[256,16384]{1,0:T(8,128)} %copy-done.2), kind=kOutput, calls=%fused_computation.50 | convolution fusion | flops 50331648 | bytes 16843776 | tf_op jit(solution)/shard_map/dot_general | solution.py:68
  152.2 30.5 %all_gather.10 = bf16[256,256]{1,0:T(8,128)(2,1)S(1)} all-gather(bf16[32,256]{1,0:T(8,128)(2,1)S(1)} %get-tuple-element.13), channel_id=1, replica_groups=mesh['patch'=4,'proto'=8] {'proto'}, dimensions={0}, use_global_device_ids=true | all-gather | bytes 147456 | tf_op jit(solution)/shard_map/all_gather | solution.py:59
  183.6 16.1 %fusion.24 = f32[1,256]{1,0:T(1,128)S(1)} fusion(f32[256,16384]{1,0:T(8,128)} %copy-done.2, f32[16384,1]{0,1:T(1,128)S(1)} %bitcast.33), kind=kOutput, calls=%fused_computation.51 | convolution fusion | flops 50331648 | bytes 16843776 | tf_op jit(solution)/shard_map/dot_general | solution.py:70
  199.6 18.5 %psum.74 = f32[256]{0:T(256)S(1)} all-reduce(f32[256]{0:T(256)S(1)} %bitcast.37), channel_id=1, replica_groups=mesh['patch'=4,'proto'=8] {'proto'}, use_global_device_ids=true, to_apply=%region_8.10 | all-reduce | flops 256 | bytes 2048 | tf_op jit(solution)/shard_map/psum | solution.py:71
  218.1 12.1 %fusion.25 = f32[1,16384]{1,0:T(1,128)} fusion(f32[256,1]{0,1:T(1,128)S(1)} %bitcast.38, f32[256,16384]{1,0:T(8,128)} %copy-done.2), kind=kOutput, calls=%fused_computation.52 | convolution fusion | flops 50331648 | bytes 16843776 | tf_op jit(solution)/shard_map/dot_general | solution.py:68
  230.3 12.7 %exponential_reduce_fusion = (f32[256]{0:T(256)S(1)}, f32[256,16384]{1,0:T(8,128)}) fusion(bf16[256,256]{1,0:T(8,128)(2,1)S(1)} %all_gather.10, f32[16384]{0:T(1024)S(1)} %add_rsqrt_fusion, bf16[256,16384]{1,0:T(8,128)(2,1)} %param.9), kind=kOutput, calls=%fused_computation.12 | convolution fusion | flops 2168454912 | bytes 25363456 | tf_op jit(solution)/shard_map/dot_general | solution.py:72
  244.5 18.0 %all-reduce = bf16[256]{0:T(256)(128)(2,1)S(1)} all-reduce(bf16[256]{0:T(256)(128)(2,1)S(1)} %dynamic-update-slice), channel_id=1, replica_groups=mesh['patch'=4,'proto'=8] {'proto'}, use_global_device_ids=true, to_apply=%add | all-reduce | flops 256 | bytes 1024
  263.4 16.1 %fusion.26 = f32[1,256]{1,0:T(1,128)S(1)} fusion(f32[256,16384]{1,0:T(8,128)} %copy-done.2, f32[16384,1]{0,1:T(1,128)S(1)} %bitcast.28), kind=kOutput, calls=%fused_computation.53 | convolution fusion | flops 50331648 | bytes 16843776 | tf_op jit(solution)/shard_map/dot_general | solution.py:70
  279.4 18.6 %all-reduce.2 = (f32[256]{0:T(256)S(1)}, f32[256]{0:T(256)S(1)}) all-reduce(f32[256]{0:T(256)S(1)} %bitcast.34, f32[256]{0:T(256)S(1)} %get-tuple-element.14), channel_id=1, replica_groups=mesh['patch'=4,'proto'=8] {'proto'}, use_global_device_ids=true, to_apply=%region_10.12 | all-reduce | flops 512 | bytes 4096 | tf_op jit(solution)/shard_map/psum | solution.py:71
  298.0 13.6 %multiply_reduce_fusion = (f32[]{:T(128)}, bf16[256,16384]{1,0:T(8,128)(2,1)S(1)}) fusion(f32[256,16384]{1,0:T(8,128)} %get-tuple-element.15, f32[256,16384]{1,0:T(8,128)} %copy-done.2, f32[256]{0:T(256)S(1)} %log.3, f32[16384]{0:T(1024)S(1)} %broadcast_divide_fusion, f32[256]{0:T(256)S(1)} %broadcast_divide_fusion.5, f32[256]{0:T(256)S(1)} %convert_element_type.28, ...), kind=kLoop, calls=%fused_computation.9 | loop fusion | flops 41943040 | bytes 42012676 | tf_op jit(solution)/shard_map/reduce_sum | solution.py:25
  314.8 6.5 %fusion.7 = f32[256,256]{1,0:T(8,128)} fusion(bf16[256,16384]{1,0:T(8,128)(2,1)S(1)} %get-tuple-element.11, f32[16384]{0:T(1024)S(1)} %add_rsqrt_fusion, bf16[256,16384]{1,0:T(8,128)(2,1)} %param.9), kind=kOutput, calls=%fused_computation.17 | convolution fusion | flops 2160132096 | bytes 17104896 | tf_op jit(solution)/shard_map/dot_general | solution.py:31
  321.4 11.5 %convolution_multiply_fusion = f32[256,16384]{1,0:T(8,128)} fusion(bf16[256,256]{1,0:T(8,128)(2,1)S(1)} %all_gather.10, bf16[256,16384]{1,0:T(8,128)(2,1)} %copy-done.3), kind=kOutput, calls=%fused_computation.2 | convolution fusion | flops 2151677952 | bytes 25296896 | tf_op jit(solution)/shard_map/dot_general | solution.py:40
  333.6 11.2 %convert_multiply_fusion = f32[256,16384]{1,0:T(8,128)} fusion(bf16[256,16384]{1,0:T(8,128)(2,1)} %param.9, f32[16384]{0:T(1024)S(1)} %add_rsqrt_fusion), kind=kLoop, calls=%fused_computation.6 | loop fusion | flops 8388608 | bytes 25231360 | tf_op jit(solution)/shard_map/mul | solution.py:55
  344.8 37.2 %all-reduce.1 = (f32[]{:T(128)}, f32[]{:T(128)}) all-reduce(f32[]{:T(128)} %get-tuple-element.10, f32[]{:T(128)} %convert_reduce_fusion), channel_id=1, replica_groups=mesh['patch'=4,'proto'=8] {'patch','proto'}, use_global_device_ids=true, to_apply=%region_17.19 | all-reduce | flops 2 | bytes 16 | tf_op jit(solution)/shard_map/psum | solution.py:89
  384.3 122.8 %reduce-scatter.5.cloned.1.call-done = f32[64,16384]{1,0:T(8,128)} async-done(((f32[256,16384]{1,0:T(8,128)}), f32[64,16384]{1,0:T(8,128)}) %reduce-scatter.5.cloned.1.call-update) | async-done | bytes 4194320 | tf_op jit(solution)/shard_map/reduce_scatter | solution.py:83
  513.3 29.8 %all-reduce.14.cloned.1.call-done = f32[16384]{0:T(1024)} async-done(((f32[16384]{0:T(1024)}), f32[16384]{0:T(1024)}) %all-reduce.14.cloned.1.call-update) | async-done | bytes 65552 | tf_op jit(solution)/shard_map/psum | solution.py:87
  543.1 6.0 %subtract_multiply_fusion = f32[64,16384]{1,0:T(8,128)} fusion(f32[64,16384]{1,0:T(8,128)} %reduce-scatter.5.cloned.1.call-done, f32[256,16384]{1,0:T(8,128)} %convert_multiply_fusion, s32[]{:T(128)S(6)} %select_n.10, f32[16384]{0:T(1024)} %all-reduce.14.cloned.1.call-done, f32[16384]{0:T(1024)S(1)} %add_rsqrt_fusion), kind=kLoop, calls=%fused_computation.13 | loop fusion | flops 3145728 | bytes 12713988 | tf_op jit(solution)/shard_map/mul | solution.py:88
  (51 shorter events, 23.6 us)
Async XLA Ops:
  7.2 1.4 copy-start
  7.2 94.4 %all-reduce.8.cloned.1.call-start = ((), (), s32[]{:S(2)}) async-start(), calls=%async_computation.2 | async-start | bytes 131072 | tf_op jit(solution)/shard_map/psum | solution.py:69
  55.2 5.7 %copy-start.2 = (f32[256,16384]{1,0:T(8,128)}, f32[256,16384]{1,0:T(8,128)S(1)}, u32[]{:S(2)}) copy-start(f32[256,16384]{1,0:T(8,128)S(1)} %fusion) | copy-start | bytes 50331652
  69.5 113.3 %all-reduce.10.cloned.1.call-start = ((), (), s32[]{:S(2)}) async-start(), calls=%async_computation.3 | async-start | bytes 131072 | tf_op jit(solution)/shard_map/psum | solution.py:69
  152.1 110.3 %all-reduce.12.cloned.1.call-start = ((), (), s32[]{:S(2)}) async-start(), calls=%async_computation.4 | async-start | bytes 131072 | tf_op jit(solution)/shard_map/psum | solution.py:69
  230.2 12.8 %copy-start.5 = (u32[32]{0:T(128)S(1)}, u32[32]{0:T(128)}, u32[]{:S(2)}) copy-start(u32[32]{0:T(128)} %constant.40) | copy-start | bytes 388
  230.2 14.1 %copy-start.4 = (bf16[32]{0:T(256)(128)(2,1)S(1)}, bf16[32]{0:T(256)(128)(2,1)}, u32[]{:S(2)}) copy-start(bf16[32]{0:T(256)(128)(2,1)} %param.11) | copy-start | bytes 196
  230.2 153.2 %reduce-scatter.3.cloned.1.call-start = ((), (), s32[]{:S(2)}) async-start(), calls=%async_computation.5 | async-start | bytes 294912 | tf_op jit(solution)/shard_map/reduce_scatter | solution.py:78
  311.6 3.2 copy-start.3
  321.4 185.8 %reduce-scatter.5.cloned.1.call-start = ((), (), s32[]{:S(2)}) async-start(), calls=%async_computation.6 | async-start | bytes 20971520 | tf_op jit(solution)/shard_map/reduce_scatter | solution.py:83
  332.9 210.1 %all-reduce.14.cloned.1.call-start = ((), (), s32[]{:S(2)}) async-start(), calls=%async_computation.7 | async-start | bytes 131072 | tf_op jit(solution)/shard_map/psum | solution.py:87
  333.6 215.4 %copy-start.1 = (bf16[256,256]{1,0:T(8,128)(2,1)S(1)}, bf16[256,256]{1,0:T(8,128)(2,1)}, u32[]{:S(2)}) copy-start(bf16[256,256]{1,0:T(8,128)(2,1)} %param.7) | copy-start | bytes 393220
Sparse Core Ops, SparseCore 0:
  69.6 31.9 all-reduce.7
  152.3 27.3 all-reduce.9
  230.3 27.6 all-reduce.11
  321.5 57.8 reduce-scatter.2
  382.0 125.1 reduce-scatter.4
  511.9 31.0 all-reduce.13
where the time goes:
time: 560 us; the launch traced here: 557 us
  waiting for transfers between devices  185 us (33%)
  blocking collectives  176 us (31%)
  matrix products  118 us (21%)
  other arithmetic  47.8 us (9%)
  between operations  17.6 us (3%)
  local copies, waits for them, and re-layouts  11.9 us (2%)
    reduce_scatter x1, waiting for transfers between devices, on_device(): lax.psum_scatter(head_term(student_rows, grad_logits), 'patch', scatter_d...  123 us
    psum x3, blocking collectives, on_device(): scale_rows = 1.0 / lax.psum(row_part, 'proto')  58.4 us
    dot_general x3, matrix products, on_device(): row_part = jnp.dot(teacher_exp, scale_cols, precision=highest)  48.4 us
    psum x1, blocking collectives, on_device(): lax.psum((loss_partial, jnp.sum(row_weight.astype(jnp.float32))), ('patch...  37.2 us
    dot_general x3, matrix products, on_device(): col_part = jnp.dot(scale_rows, teacher_exp, precision=highest)  32.7 us
    all_gather x1, blocking collectives, on_device(): lax.all_gather(own_teacher, 'proto', axis=0, tiled=True)  32.3 us
    psum x3, waiting for transfers between devices, on_device(): scale_cols = 1.0 / lax.psum(col_part, 'patch')  32.1 us
    all_gather x1, blocking collectives, on_device(): lax.all_gather(own_student, 'proto', axis=0, tiled=True)  30.5 us
  transfers between devices with their start and end apart: 6, of which 3 were waited for; matrix products, arithmetic and copies ran while one was open for 7% of the time, Pallas kernels for 0%

commit v1 on v0

v1 whole, which is shorter than its diff:
```python
import functools

import jax
import jax.numpy as jnp
from jax import lax
from jax.experimental import pallas as pl
from jax.experimental.pallas import tpu as pltpu
from jax.sharding import PartitionSpec as P

SK_ITERS = 3

eps = 1e-06
teacher_temp = 0.07
student_temp = 0.1
AXES = ("patch", "proto")
LANES = 128


def unit_rows(values):
    values = values.astype(jnp.float32)
    inverse = lax.rsqrt(jnp.sum(values * values, axis=1) + eps)
    return (values * inverse[:, None], inverse)


def unit_block(w_ref):
    w = w_ref[...].astype(jnp.float32)
    inverse = lax.rsqrt(jnp.sum(w * w, axis=0, keepdims=True) + eps)
    unit = w * inverse
    return unit, inverse, unit.astype(jnp.bfloat16)


def scaled_dot(rows_ref, block, temp):
    return jnp.dot(rows_ref[...], block, preferred_element_type=jnp.float32) * (1.0 / temp)


def lane_sums(values):
    total = values[:, :LANES]
    for start in range(LANES, values.shape[1], LANES):
        total = total + values[:, start : start + LANES]
    return total


def sweep_kernel(first, last, t_ref, s_ref, w_ref, r_ref, row_ref, extra_ref, c_ref, row_acc, extra_acc):
    step = pl.program_id(0)

    @pl.when(step == 0)
    def _():
        row_acc[...] = jnp.zeros_like(row_acc)
        extra_acc[...] = jnp.zeros_like(extra_acc)

    _, _, block = unit_block(w_ref)
    table = jnp.exp(scaled_dot(t_ref, block, teacher_temp))
    weighted = table if first else table * r_ref[...]
    cols = 1.0 / jnp.sum(weighted, axis=0, keepdims=True)
    c_ref[...] = cols
    part = table * cols
    row_acc[...] += lane_sums(part)
    if first:
        extra_acc[...] += lane_sums(jnp.exp(scaled_dot(s_ref, block, student_temp)))
    if last:
        extra_acc[...] += lane_sums(part * scaled_dot(s_ref, block, student_temp))

    @pl.when(step == pl.num_programs(0) - 1)
    def _():
        row_ref[...] = jnp.sum(row_acc[...], axis=1, keepdims=True)
        extra_ref[...] = jnp.sum(extra_acc[...], axis=1, keepdims=True)


def final_kernel(t_ref, s_ref, st_ref, w_ref, wr_ref, wt_ref, c_ref, feat_ref, grad_ref):
    step = pl.program_id(0)

    @pl.when(step == 0)
    def _():
        feat_ref[...] = jnp.zeros_like(feat_ref)

    unit, inverse, block = unit_block(w_ref)
    codes = jnp.exp(scaled_dot(t_ref, block, teacher_temp)) * c_ref[...] * wr_ref[...]
    probs = jnp.exp(scaled_dot(s_ref, block, student_temp)) * wt_ref[...]
    grad = (probs - codes).astype(jnp.bfloat16)
    feat_ref[...] += lax.dot_general(
        grad, block, (((1,), (1,)), ((), ())), preferred_element_type=jnp.float32
    )
    head = scaled_dot(st_ref, grad, student_temp)
    inner = jnp.sum(unit * head, axis=0, keepdims=True)
    grad_ref[...] = (inverse * (head - unit * inner)).astype(jnp.bfloat16)


def whole(shape):
    return pl.BlockSpec(shape, lambda i: (0, 0))


def split(rows, width):
    return pl.BlockSpec((rows, width), lambda i: (0, i))


def params():
    return pltpu.CompilerParams(
        dimension_semantics=("arbitrary",), vmem_limit_bytes=50 * 1024 * 1024
    )


def block_width(rows, cols):
    return min(cols, max(LANES, 262144 // rows))


def sweep(first, last, teacher, student, w_own, scale_rows):
    rows, depth = teacher.shape
    cols = w_own.shape[1]
    width = block_width(rows, cols)
    return pl.pallas_call(
        functools.partial(sweep_kernel, first, last),
        grid=(cols // width,),
        in_specs=[whole((rows, depth)), whole((rows, depth)), split(depth, width), whole((rows, 1))],
        out_specs=[whole((rows, 1)), whole((rows, 1)), split(1, width)],
        out_shape=[
            jax.ShapeDtypeStruct((rows, 1), jnp.float32),
            jax.ShapeDtypeStruct((rows, 1), jnp.float32),
            jax.ShapeDtypeStruct((1, cols), jnp.float32),
        ],
        scratch_shapes=[pltpu.VMEM((rows, LANES), jnp.float32)] * 2,
        compiler_params=params(),
    )(teacher, student, w_own, scale_rows)


def gradients(teacher, student, w_own, weight_rows, weight_total, scale_cols):
    rows, depth = teacher.shape
    cols = w_own.shape[1]
    width = block_width(rows, cols)
    return pl.pallas_call(
        final_kernel,
        grid=(cols // width,),
        in_specs=[
            whole((rows, depth)),
            whole((rows, depth)),
            whole((depth, rows)),
            split(depth, width),
            whole((rows, 1)),
            whole((rows, 1)),
            split(1, width),
        ],
        out_specs=[whole((rows, depth)), split(depth, width)],
        out_shape=[
            jax.ShapeDtypeStruct((rows, depth), jnp.float32),
            jax.ShapeDtypeStruct((depth, cols), jnp.bfloat16),
        ],
        compiler_params=params(),
    )(teacher, student, student.T, w_own, weight_rows, weight_total, scale_cols)


def on_device(student_feats, teacher_feats, proto_weight, mask_index, row_weight):
    unit_student, inverse_student = unit_rows(jnp.take(student_feats, mask_index, axis=0))
    unit_teacher, _ = unit_rows(jnp.take(teacher_feats, mask_index, axis=0))
    depth = unit_student.shape[1]
    own = jnp.concatenate(
        [
            unit_student.astype(jnp.bfloat16),
            unit_teacher.astype(jnp.bfloat16),
            jnp.broadcast_to(row_weight[:, None], (row_weight.shape[0], LANES)),
        ],
        axis=1,
    )
    rows = lax.all_gather(own, AXES, axis=0, tiled=True)
    student, teacher = rows[:, :depth], rows[:, depth : 2 * depth]
    weights = rows[:, 2 * depth : 2 * depth + 1].astype(jnp.float32)
    share = proto_weight.shape[1] // lax.axis_size("patch")
    w_own = lax.dynamic_slice_in_dim(proto_weight, lax.axis_index("patch") * share, share, 1)

    scale_rows = jnp.ones((student.shape[0], 1), jnp.float32)
    for step in range(SK_ITERS):
        first, last = step == 0, step == SK_ITERS - 1
        row_part, extra, scale_cols = sweep(first, last, teacher, student, w_own, scale_rows)
        if first or last:
            both = lax.psum(jnp.concatenate([row_part[:, 0], extra[:, 0]]), AXES)
            row_total, extra = both[: row_part.shape[0], None], both[row_part.shape[0] :, None]
        else:
            row_total = lax.psum(row_part[:, 0], AXES)[:, None]
        scale_rows = 1.0 / row_total
        if first:
            exp_total = extra
    loss = jnp.sum(weights * (jnp.log(exp_total) - scale_rows * extra)) / jnp.sum(weights)

    feature, grad_own = gradients(
        teacher, student, w_own, weights * scale_rows, weights / exp_total, scale_cols
    )
    grad_proto = lax.all_to_all(grad_own, "patch", split_axis=0, concat_axis=1, tiled=True)
    feature_grad = lax.psum_scatter(feature, AXES, scatter_dimension=0, tiled=True) / student_temp
    grad_student = inverse_student[:, None] * (
        feature_grad - unit_student * jnp.sum(unit_student * feature_grad, axis=1)[:, None]
    )
    return (grad_student, grad_proto.astype(jnp.float32), loss)


def solution(mesh):
    in_specs = (P(AXES, None), P(AXES, None), P(None, "proto"), P(AXES), P(AXES))
    out_specs = (P(AXES, None), P("patch", "proto"), P())
    return jax.shard_map(
        on_device, mesh=mesh, in_specs=in_specs, out_specs=out_specs, check_vma=False
    )
```

time: 560 us -> 411 us (0.73)
  matrix products: 118 us -> 0 us
  Pallas kernels: 0 us -> 61.3 us
  blocking collectives: 176 us -> 119 us
  other arithmetic: 47.8 us -> 6.88 us
    dot_general x10 -> x0, matrix products: 118 us -> none  [the longest x3 48.4 us: on_device(): row_part = jnp.dot(teacher_exp, scale_cols, precision=highest)]
    all_gather x2 -> x0, blocking collectives: 62.8 us -> none  [the longest x1 32.3 us: on_device(): lax.all_gather(own_teacher, 'proto', axis=0, tiled=True)]
    psum x4 -> x0, waiting for transfers between devices: 61.9 us -> none  [the longest x3 32.1 us: on_device(): scale_cols = 1.0 / lax.psum(col_part, 'patch')]
    pallas_call x0 -> x4, Pallas kernels: none -> 61.3 us  [the longest x3 43.9 us: sweep(): pl.pallas_call(functools.partial(sweep_kernel, first, last), grid=(cols /...]
    all_gather x0 -> x1, waiting for transfers between devices: none -> 54.1 us  [on_device(): rows = lax.all_gather(own, AXES, axis=0, tiled=True)]
    psum x4 -> x3, blocking collectives: 95.6 us -> 119 us  [the longest x2 79.1 us: on_device(): both = lax.psum(jnp.concatenate([row_part[:, 0], extra[:, 0]]), AXES)]
    reduce_sum x4 -> x1, other arithmetic: 24 us -> 0.61 us  [on_device(): jnp.sum(weights)]
    all_to_all x0 -> x1, waiting for transfers between devices: none -> 23 us  [on_device(): lax.all_to_all(grad_own, 'patch', split_axis=0, concat_axis=1, tiled=True)]
  transfers between devices with their start and end apart: 6 -> 3, of which waited for: 3 -> 3; matrix products, arithmetic and copies ran while one was open for 7% -> 2% of each run, Pallas kernels for 0% -> 0%
where the time goes in v1:
time: 411 us; the launch traced here: 409 us
  waiting for transfers between devices  188 us (46%)
  blocking collectives  119 us (29%)
  Pallas kernels  61.3 us (15%)
  between operations  16.7 us (4%)
  local copies, waits for them, and re-layouts  12.8 us (3%)
  other arithmetic  6.88 us (2%)
    reduce_scatter x1, waiting for transfers between devices, on_device(): lax.psum_scatter(feature, AXES, scatter_dimension=0, tiled=True)  110 us
    psum x2, blocking collectives, on_device(): both = lax.psum(jnp.concatenate([row_part[:, 0], extra[:, 0]]), AXES)  79.1 us
    all_gather x1, waiting for transfers between devices, on_device(): rows = lax.all_gather(own, AXES, axis=0, tiled=True)  54.1 us
    pallas_call x3, Pallas kernels, sweep(): pl.pallas_call(functools.partial(sweep_kernel, first, last), grid=(cols /...  43.9 us
    psum x1, blocking collectives, on_device(): row_total = lax.psum(row_part[:, 0], AXES)[:, None]  40.2 us
    all_to_all x1, waiting for transfers between devices, on_device(): lax.all_to_all(grad_own, 'patch', split_axis=0, concat_axis=1, tiled=True)  23 us
    pallas_call x1, Pallas kernels, gradients(): pl.pallas_call(final_kernel, grid=(cols // width,), in_specs=[whole((rows...  17.5 us
  transfers between devices with their start and end apart: 3, of which 3 were waited for; matrix products, arithmetic and copies ran while one was open for 2% of the time, Pallas kernels for 0%

profile of v1, /device:TPU:0, one launch (start us, length us, event | category | flops | bytes accessed | tf_op | source)
XLA Modules:
  0.0 409.0 jit_solution(15403891811988301511)
XLA Ops:
  7.2 0.7 compare_and_fusion
  7.9 0.7 compare_select_fusion
  8.6 0.6 gather_fusion
  9.2 1.5 gather_fusion.1
  11.0 0.7 broadcast_in_dim.13
  12.4 3.1 constant_dynamic-slice_fusion.w_ref
  15.5 54.1 %all-gather.2.cloned.1.call-done = bf16[1024,640]{1,0:T(8,128)(2,1)} async-done(((bf16[32,640]{1,0:T(8,128)(2,1)}), bf16[1024,640]{1,0:T(8,128)(2,1)}) %all-gather.2.cloned.1.call-update) | async-done | bytes 1310736 | tf_op jit(solution)/shard_map/all_gather | solution.py:162
  69.7 1.0 slice.34
  70.8 1.3 fusion.10
  72.3 1.0 copy.43
  73.3 14.3 %shard_map.76 = (f32[1024,1]{1,0:T(8,128)S(1)}, f32[1024,1]{1,0:T(8,128)S(1)}, f32[1,4096]{1,0:T(1,128)}) custom-call(bf16[1024,256]{1,0:T(8,128)(2,1)S(1)} %get-tuple-element.28.t_ref, bf16[1024,256]{1,0:T(8,128)(2,1)S(1)} %get-tuple-element.27.s_ref, bf16[256,4096]{1,0:T(8,128)(2,1)} %constant_dynamic-slice_fusion.w_ref, f32[1024,1]{1,0:T(8,128)S(1)} %broadcast_2_r_ref.2.r_ref), custom_call_target="tpu_custom_call" | custom-call | tf_op jit(solution)/shard_map/pallas_call | solution.py:110
  88.0 39.2 %psum.21 = f32[2048]{0:T(1024)S(1)} all-reduce(f32[2048]{0:T(1024)S(1)} %pad_maximum_fusion.1), channel_id=1, replica_groups=mesh['patch'=4,'proto'=8] {'patch','proto'}, use_global_device_ids=true, to_apply=%region_2.4 | all-reduce | flops 2048 | bytes 16384 | tf_op jit(solution)/shard_map/psum | solution.py:173
  127.4 14.1 %shard_map.77 = (f32[1024,1]{1,0:T(8,128)S(1)}, f32[1024,1]{1,0:T(8,128)}, f32[1,4096]{1,0:T(1,128)}) custom-call(bf16[1024,256]{1,0:T(8,128)(2,1)S(1)} %get-tuple-element.28.t_ref, bf16[1024,256]{1,0:T(8,128)(2,1)S(1)} %get-tuple-element.27.s_ref, bf16[256,4096]{1,0:T(8,128)(2,1)} %constant_dynamic-slice_fusion.w_ref, f32[1024,1]{1,0:T(8,128)S(1)} %copy.40.r_ref), custom_call_target="tpu_custom_call" | custom-call | tf_op jit(solution)/shard_map/pallas_call | solution.py:110
  141.8 40.2 %psum.22 = f32[1024]{0:T(1024)S(1)} all-reduce(f32[1024]{0:T(1024)S(1)} %reduce.2), channel_id=1, replica_groups=mesh['patch'=4,'proto'=8] {'patch','proto'}, use_global_device_ids=true, to_apply=%region_3.5 | all-reduce | flops 1024 | bytes 8192 | tf_op jit(solution)/shard_map/psum | solution.py:176
  182.2 15.5 %shard_map.78 = (f32[1024,1]{1,0:T(8,128)S(1)}, f32[1024,1]{1,0:T(8,128)S(1)}, f32[1,4096]{1,0:T(1,128)S(1)}) custom-call(bf16[1024,256]{1,0:T(8,128)(2,1)S(1)} %get-tuple-element.28.t_ref, bf16[1024,256]{1,0:T(8,128)(2,1)S(1)} %get-tuple-element.27.s_ref, bf16[256,4096]{1,0:T(8,128)(2,1)} %constant_dynamic-slice_fusion.w_ref, f32[1024,1]{1,0:T(8,128)S(1)} %copy.42.r_ref), custom_call_target="tpu_custom_call" | custom-call | tf_op jit(solution)/shard_map/pallas_call | solution.py:110
  198.1 39.9 %psum.23 = f32[2048]{0:T(1024)S(1)} all-reduce(f32[2048]{0:T(1024)S(1)} %pad_maximum_fusion.2), channel_id=1, replica_groups=mesh['patch'=4,'proto'=8] {'patch','proto'}, use_global_device_ids=true, to_apply=%region_4.6 | all-reduce | flops 2048 | bytes 16384 | tf_op jit(solution)/shard_map/psum | solution.py:173
  238.6 17.5 %shard_map.79 = (f32[1024,256]{1,0:T(8,128)}, bf16[256,4096]{1,0:T(8,128)(2,1)}) custom-call(bf16[1024,256]{1,0:T(8,128)(2,1)S(1)} %get-tuple-element.28.t_ref, bf16[1024,256]{1,0:T(8,128)(2,1)S(1)} %get-tuple-element.27.s_ref, bf16[256,1024]{1,0:T(8,128)(2,1)S(1)} %bitcast.12, bf16[256,4096]{1,0:T(8,128)(2,1)} %constant_dynamic-slice_fusion.w_ref, ...), custom_call_target="tpu_custom_call" | custom-call | tf_op jit(solution)/shard_map/pallas_call | solution.py:129
  256.1 3.6 all-to-all-start
  259.7 0.7 reduce-scatter.4.cloned.1.call-update
  262.4 23.0 %all-to-all-done = bf16[4,64,4096]{2,1,0:T(8,128)(2,1)S(1)} async-done(((bf16[4,64,4096]{2,1,0:T(8,128)(2,1)}), bf16[4,64,4096]{2,1,0:T(8,128)(2,1)S(1)}, u32[]{:S(2)}, u32[]{:S(2)}) %all-to-all-start) | async-done | bytes 2097184 | tf_op jit(solution)/shard_map/all_to_all | solution.py:185
  285.8 2.3 copy.55
  288.1 110.5 %reduce-scatter.4.cloned.1.call-done = f32[32,256]{1,0:T(8,128)} async-done(((f32[1024,256]{1,0:T(8,128)}), f32[32,256]{1,0:T(8,128)}) %reduce-scatter.4.cloned.1.call-update) | async-done | bytes 32784 | tf_op jit(solution)/shard_map/reduce_scatter | solution.py:186
  398.6 0.9 fusion.3
  399.6 1.5 fusion.5
  (32 shorter events, 4.5 us)
Async XLA Ops:
  7.2 1.4 copy-start
  7.2 62.5 %all-gather.2.cloned.1.call-start = ((), (), s32[]{:S(2)}) async-start(), calls=%async_computation.2 | async-start | bytes 1351680 | tf_op jit(solution)/shard_map/all_gather | solution.py:162
  197.7 40.8 %copy-start.1 = (f32[1024,1]{1,0:T(8,128)S(1)}, f32[1024,1]{1,0:T(8,128)}, u32[]{:S(2)}) copy-start(f32[1024,1]{1,0:T(8,128)} %copy.43) | copy-start | bytes 12292
  256.1 29.3 %all-to-all-start = ((bf16[4,64,4096]{2,1,0:T(8,128)(2,1)}), bf16[4,64,4096]{2,1,0:T(8,128)(2,1)S(1)}, u32[]{:S(2)}, u32[]{:S(2)}) async-start(bf16[4,64,4096]{2,1,0:T(8,128)(2,1)} %bitcast.14), calls=%async_computation | async-start | bytes 4194304 | tf_op jit(solution)/shard_map/all_to_all | solution.py:185
  259.7 139.0 %reduce-scatter.4.cloned.1.call-start = ((), (), s32[]{:S(2)}) async-start(), calls=%async_computation.3 | async-start | bytes 1081344 | tf_op jit(solution)/shard_map/reduce_scatter | solution.py:186
Sparse Core Ops, SparseCore 0:
  12.5 57.0 all-gather.1
  262.8 135.8 reduce-scatter.3
